TPU v7x, 32 devices: a whole 2x2x4 slice. The times are simulated.
32 devices in a mesh: groups: 2 (over y), tm: 8 (over z, x), head: 2 (over core).
Axes of the slice: x: 2, y: 2, z: 4, core: 2. Of those that a mesh axis runs over, the one named last changes fastest.
Arguments:
- queries: bfloat16 [4096, 2560], P(('groups', 'tm'), 'head'), parts along dimension 0, may hold values from -2.5 to 2.5
- keys: bfloat16 [4096, 2560], P(('groups', 'tm'), 'head'), parts along dimension 0, may hold values from -2.5 to 2.5
- values: bfloat16 [4096, 2560], P(('groups', 'tm'), 'head'), parts along dimension 0, may hold values from -6 to 6
- out_grad: bfloat16 [4096, 2560], P(('groups', 'tm'), 'head'), parts along dimension 0, may hold values from -6 to 6
- pair_mask: int32 [16, 5], P('groups'), parts along dimension 0, may hold values from 0 to 1, as said below
Outputs:
- query_grad: bfloat16 [4096, 2560], P(('groups', 'tm'), 'head'), parts along dimension 0
- key_grad: bfloat16 [4096, 2560], P(('groups', 'tm'), 'head'), parts along dimension 0
- value_grad: bfloat16 [4096, 2560], P(('groups', 'tm'), 'head'), parts along dimension 0
There are 2 independent parts, one for each index of `groups`. A program takes and returns all parts, laid end to end along the dimension named above; each array names one. Nothing has to cross between parts.
Inputs may be any that keep to these rules, and one draw needn't show every extreme that they name: pair_mask[f, s] is 1 where query frame f attends the key frame of slot s. It is 1 for slot 0 and for offsets 1 and -1 wherever the key frame lies inside the video, and 0 wherever the key frame lies outside it.
All inputs are finite; a program needn't handle non-finite values.
Results may differ from a plain program's by a relative error of at most 0.0062.
Values may be sent and summed in bfloat16 or wider, within the bound.
A program may use at most 64 MiB of HBM per device.

v0:
```python
from functools import partial

import jax
import jax.numpy as jnp
from jax import lax
from jax.sharding import PartitionSpec as P

HDIM = 128
DISTANCE_LEVELS = 2


def shifted(value, axis, by):
    devices = lax.axis_size(axis)
    pairs = [(i, i + by) for i in range(devices) if 0 <= i + by < devices]
    return lax.ppermute(value, axis, pairs)


def slot_offsets(levels):
    offsets = [0]
    for level_index in range(levels):
        offsets = offsets + [2**level_index, -(2**level_index)]
    return offsets


def scores_of(query_heads, key_heads, score_scale):
    return (
        jnp.einsum("qhd,khd->hqk", query_heads, key_heads, preferred_element_type=jnp.float32)
        * score_scale
    )


def forward_terms(query_heads, key_heads, value_heads, live_flag, score_scale):
    attention_weights = jnp.exp(scores_of(query_heads, key_heads, score_scale)) * live_flag
    part_total = jnp.sum(attention_weights, axis=2)
    part_numerator = jnp.einsum(
        "hqk,khd->qhd",
        attention_weights.astype(jnp.bfloat16),
        value_heads,
        preferred_element_type=jnp.float32,
    )
    return (part_total, part_numerator)


def backward_terms(
    query_heads,
    grad_heads,
    key_heads,
    value_heads,
    row_total,
    row_delta,
    live_flag,
    score_scale,
    want_query,
    want_key,
):
    probabilities = (
        jnp.exp(scores_of(query_heads, key_heads, score_scale)) * live_flag / row_total[:, :, None]
    )
    dprobs = jnp.einsum("qhd,khd->hqk", grad_heads, value_heads, preferred_element_type=jnp.float32)
    dscores = (probabilities * (dprobs - row_delta[:, :, None])).astype(jnp.bfloat16)
    results = []
    results.append(
        jnp.einsum("hqk,khd->qhd", dscores, key_heads, preferred_element_type=jnp.float32)
    )
    key_term = (
        jnp.einsum("hqk,qhd->khd", dscores, query_heads, preferred_element_type=jnp.float32)
        * score_scale
    ).astype(jnp.bfloat16)
    value_term = jnp.einsum(
        "hqk,qhd->khd",
        probabilities.astype(jnp.bfloat16),
        grad_heads,
        preferred_element_type=jnp.float32,
    ).astype(jnp.bfloat16)
    results.append(jnp.stack([key_term, value_term]))
    return tuple(results)


def shards(queries, keys, values, out_grad, pair_mask):
    row_count = queries.shape[0]
    head_count = queries.shape[1] // HDIM
    score_scale = HDIM ** (-0.5)
    tm_width = lax.axis_size("tm")
    own_frame = lax.axis_index("tm")
    head_shape = (row_count, head_count, HDIM)
    query_heads = queries.reshape(head_shape)
    grad_heads = out_grad.reshape(head_shape)
    offsets = slot_offsets(DISTANCE_LEVELS)
    live_slots = [
        slot_index for slot_index in range(len(offsets)) if abs(offsets[slot_index]) < tm_width
    ]
    own_pair = jnp.stack([keys, values])
    fetched = []
    live_flags = []
    for slot_index in live_slots:
        shift_by = offsets[slot_index]
        if shift_by == 0:
            fetched.append(own_pair)
        else:
            fetched.append(shifted(own_pair, "tm", -shift_by))
        live_flags.append(pair_mask[own_frame, slot_index].astype(jnp.float32))
    row_total = jnp.zeros((head_count, row_count), jnp.float32)
    numerator = jnp.zeros(head_shape, jnp.float32)
    for position in range(len(live_slots)):
        remote = fetched[position]
        compute = partial(
            forward_terms,
            query_heads,
            remote[0].reshape(head_shape),
            remote[1].reshape(head_shape),
            live_flags[position],
            score_scale,
        )
        part_total, part_numerator = compute()
        row_total = row_total + part_total
        numerator = numerator + part_numerator
    row_delta = jnp.transpose(
        jnp.sum(
            grad_heads.astype(jnp.float32) * (numerator / jnp.transpose(row_total)[:, :, None]),
            axis=2,
        )
    )
    query_sum = jnp.zeros(head_shape, jnp.float32)
    pair_sum = jnp.zeros((2,) + head_shape, jnp.float32)
    for position, slot_index in enumerate(live_slots):
        remote = fetched[position]
        compute = partial(
            backward_terms,
            query_heads,
            grad_heads,
            remote[0].reshape(head_shape),
            remote[1].reshape(head_shape),
            row_total,
            row_delta,
            live_flags[position],
            score_scale,
            True,
            True,
        )
        query_term, pairwise_term = compute()
        query_sum = query_sum + query_term
        shift_by = offsets[slot_index]
        if shift_by != 0:
            pairwise_term = shifted(pairwise_term, "tm", shift_by)
        pair_sum = pair_sum + lax.optimization_barrier(pairwise_term).astype(jnp.float32)
    flat_shape = (row_count, head_count * HDIM)
    query_grad = (query_sum * score_scale).astype(jnp.bfloat16).reshape(flat_shape)
    key_grad = pair_sum[0].astype(jnp.bfloat16).reshape(flat_shape)
    value_grad = pair_sum[1].astype(jnp.bfloat16).reshape(flat_shape)
    return (query_grad, key_grad, value_grad)


def solution(mesh):
    placed = (
        P(("groups", "tm"), "head"),
        P(("groups", "tm"), "head"),
        P(("groups", "tm"), "head"),
        P(("groups", "tm"), "head"),
        P("groups", None),
    )
    return jax.shard_map(
        shards,
        mesh=mesh,
        in_specs=placed,
        out_specs=(
            P(("groups", "tm"), "head"),
            P(("groups", "tm"), "head"),
            P(("groups", "tm"), "head"),
        ),
        check_vma=False,
    )
```

profile of v0, /device:TPU:0, one launch (start us, length us, event | category | flops | bytes accessed | tf_op | source)
XLA Modules:
  0.0 158.0 jit_solution(6926844038003123785)
XLA Ops:
  0.6 1.4 copy.59
  2.3 1.2 pad_maximum_fusion
  3.5 6.1 %collective-permute-start.3 = (bf16[2,256,1280]{1,2,0:T(8,128)(2,1)}, bf16[2,256,1280]{1,2,0:T(8,128)(2,1)}, u32[]{:S(2)}, u32[]{:S(2)}) collective-permute-start(bf16[2,256,1280]{1,2,0:T(8,128)(2,1)} %pad_maximum_fusion), channel_id=1, source_target_pairs={{0,4},{2,6},{4,8},{6,10},{8,12},{10,14},{1,5},{3,7},{5,9},{7,11},{... | collective-permute-start | bytes 3932168 | tf_op jit(solution)/shard_map/ppermute | solution.py:15
  9.6 1.3 collective-permute-start.2
  10.9 4.5 %collective-permute-start.1 = (bf16[2,256,1280]{1,2,0:T(8,128)(2,1)}, bf16[2,256,1280]{1,2,0:T(8,128)(2,1)}, u32[]{:S(2)}, u32[]{:S(2)}) collective-permute-start(bf16[2,256,1280]{1,2,0:T(8,128)(2,1)} %pad_maximum_fusion), channel_id=1, source_target_pairs={{0,2},{2,4},{4,6},{6,8},{8,10},{10,12},{12,14},{1,3},{3,5},{5,7},{... | collective-permute-start | bytes 3932168 | tf_op jit(solution)/shard_map/ppermute | solution.py:15
  15.4 1.3 collective-permute-start
  16.7 0.7 constant_dynamic-slice_fusion.3
  21.2 0.7 fusion.57
  22.3 14.6 %collective-permute-done.3 = bf16[2,256,1280]{1,2,0:T(8,128)(2,1)} collective-permute-done((bf16[2,256,1280]{1,2,0:T(8,128)(2,1)}, bf16[2,256,1280]{1,2,0:T(8,128)(2,1)}, u32[]{:S(2)}, u32[]{:S(2)}) %collective-permute-start.3) | collective-permute-done | bytes 1310752 | tf_op jit(solution)/shard_map/ppermute | solution.py:15
  36.9 1.4 fusion.56
  38.3 5.3 %collective-permute-done.2 = bf16[2,256,1280]{1,2,0:T(8,128)(2,1)} collective-permute-done((bf16[2,256,1280]{1,2,0:T(8,128)(2,1)}, bf16[2,256,1280]{1,2,0:T(8,128)(2,1)}, u32[]{:S(2)}, u32[]{:S(2)}) %collective-permute-start.2) | collective-permute-done | bytes 1310752 | tf_op jit(solution)/shard_map/ppermute | solution.py:15
  43.5 1.4 fusion.55
  44.9 0.7 bitcast_reduce_fusion
  45.6 0.7 bitcast_reduce_fusion.1
  46.4 24.1 %collective-permute-done.1 = bf16[2,256,1280]{1,2,0:T(8,128)(2,1)} collective-permute-done((bf16[2,256,1280]{1,2,0:T(8,128)(2,1)}, bf16[2,256,1280]{1,2,0:T(8,128)(2,1)}, u32[]{:S(2)}, u32[]{:S(2)}) %collective-permute-start.1) | collective-permute-done | bytes 1310752 | tf_op jit(solution)/shard_map/ppermute | solution.py:15
  70.4 1.4 fusion.54
  71.8 0.7 bitcast_reduce_fusion.2
  72.6 1.4 fusion.53
  73.9 0.7 bitcast_reduce_fusion.3
  75.8 0.5 fusion.32
  76.3 0.6 fusion.47
  76.9 0.6 multiply_convert_fusion
  77.5 0.6 fusion.3
  78.2 0.5 fusion.35
  78.7 0.5 fusion.38
  79.2 0.6 fusion.2
  79.8 0.5 fusion.41
  80.4 0.6 fusion.1
  81.0 0.5 fusion.44
  81.5 0.6 fusion
  82.1 0.5 fusion.31
  82.6 0.6 convolution_bitcast_fusion
  83.3 0.5 fusion.30
  84.0 5.5 %collective-permute-start.4 = (bf16[2,256,10,128]{3,1,2,0:T(8,128)(2,1)S(1)}, bf16[2,256,10,128]{3,1,2,0:T(8,128)(2,1)}, u32[]{:S(2)}, u32[]{:S(2)}) collective-permute-start(bf16[2,256,10,128]{3,1,2,0:T(8,128)(2,1)S(1)} %pad_maximum_fusion.2), channel_id=1, source_target_pairs={{0,2},{2,4},{4,6},{6,8},{8,10},{10,12},{12,14},{1,3},{3,5},{5,7},{... | collective-permute-start | bytes 3932168 | tf_op jit(solution)/shard_map/ppermute | solution.py:15
  89.4 0.5 fusion.29
  89.9 1.2 pad_maximum_fusion.3
  91.2 1.3 collective-permute-start.5
  93.0 1.2 pad_maximum_fusion.4
  94.1 7.3 %collective-permute-start.6 = (bf16[2,256,10,128]{3,1,2,0:T(8,128)(2,1)}, bf16[2,256,10,128]{3,1,2,0:T(8,128)(2,1)}, u32[]{:S(2)}, u32[]{:S(2)}) collective-permute-start(bf16[2,256,10,128]{3,1,2,0:T(8,128)(2,1)} %pad_maximum_fusion.4), channel_id=1, source_target_pairs={{0,4},{2,6},{4,8},{6,10},{8,12},{10,14},{1,5},{3,7},{5,9},{7,11},{... | collective-permute-start | bytes 3932168 | tf_op jit(solution)/shard_map/ppermute | solution.py:15
  102.0 1.3 pad_maximum_fusion.5
  103.2 1.3 collective-permute-start.7
  105.5 0.6 fusion.15
  106.1 1.1 copy.108
  107.2 32.7 %collective-permute-done.4 = bf16[2,256,10,128]{3,1,2,0:T(8,128)(2,1)} collective-permute-done((bf16[2,256,10,128]{3,1,2,0:T(8,128)(2,1)S(1)}, bf16[2,256,10,128]{3,1,2,0:T(8,128)(2,1)}, u32[]{:S(2)}, u32[]{:S(2)}) %collective-permute-start.4) | collective-permute-done | bytes 1310752 | tf_op jit(solution)/shard_map/ppermute | solution.py:15
  139.9 11.8 %collective-permute-done.7 = bf16[2,256,10,128]{3,1,2,0:T(8,128)(2,1)} collective-permute-done((bf16[2,256,10,128]{3,1,2,0:T(8,128)(2,1)}, bf16[2,256,10,128]{3,1,2,0:T(8,128)(2,1)}, u32[]{:S(2)}, u32[]{:S(2)}) %collective-permute-start.7) | collective-permute-done | bytes 1310752 | tf_op jit(solution)/shard_map/ppermute | solution.py:15
  151.7 3.6 %add_convert_fusion = bf16[2,256,10,128]{3,1,2,0:T(8,128)(2,1)S(1)} fusion(bf16[2,256,10,128]{3,1,2,0:T(8,128)(2,1)} %collective-permute-done.7, bf16[2,256,10,128]{3,1,2,0:T(8,128)(2,1)} %collective-permute-done.6, bf16[2,256,10,128]{3,1,2,0:T(8,128)(2,1)} %collective-permute-done.5, bf16[2,256,10,128]{3,1,2,0:T(8,128)(2,1)} %collective-permute-done.4, ...), kind=kLoop, calls=%fused_computation.20 | loop fusion | flops 6553600 | bytes 7864320 | tf_op jit(solution)/shard_map/convert.1
  155.6 1.1 copy.109
  156.9 1.1 copy.110
  (29 shorter events, 5.0 us)
Async XLA Ops:
  0.6 1.4 copy-start
  2.3 14.4 %copy-start.3 = (s32[8,5]{1,0:T(8,128)S(1)}, s32[8,5]{1,0:T(8,128)}, u32[]{:S(2)}) copy-start(s32[8,5]{1,0:T(8,128)} %param.9) | copy-start | bytes 484
  2.3 15.7 %copy-start.1 = (bf16[256,1280]{1,0:T(8,128)(2,1)S(1)}, bf16[256,1280]{1,0:T(8,128)(2,1)}, u32[]{:S(2)}) copy-start(bf16[256,1280]{1,0:T(8,128)(2,1)} %param.5) | copy-start | bytes 1966084
  3.5 17.4 %copy-start.2 = (bf16[256,1280]{1,0:T(8,128)(2,1)S(1)}, bf16[256,1280]{1,0:T(8,128)(2,1)}, u32[]{:S(2)}) copy-start(bf16[256,1280]{1,0:T(8,128)(2,1)} %param.8) | copy-start | bytes 1966084
  3.5 33.4 %collective-permute-start.3 = (bf16[2,256,1280]{1,2,0:T(8,128)(2,1)}, bf16[2,256,1280]{1,2,0:T(8,128)(2,1)}, u32[]{:S(2)}, u32[]{:S(2)}) collective-permute-start(bf16[2,256,1280]{1,2,0:T(8,128)(2,1)} %pad_maximum_fusion), channel_id=1, source_target_pairs={{0,4},{2,6},{4,8},{6,10},{8,12},{10,14},{1,5},{3,7},{5,9},{7,11},{... | collective-permute-start | bytes 3932168 | tf_op jit(solution)/shard_map/ppermute | solution.py:15
  9.6 33.9 %collective-permute-start.2 = (bf16[2,256,1280]{1,2,0:T(8,128)(2,1)}, bf16[2,256,1280]{1,2,0:T(8,128)(2,1)}, u32[]{:S(2)}, u32[]{:S(2)}) collective-permute-start(bf16[2,256,1280]{1,2,0:T(8,128)(2,1)} %pad_maximum_fusion), channel_id=1, source_target_pairs={{4,0},{6,2},{8,4},{10,6},{12,8},{14,10},{5,1},{7,3},{9,5},{11,7},{... | collective-permute-start | bytes 3932168 | tf_op jit(solution)/shard_map/ppermute | solution.py:15
  10.9 59.5 %collective-permute-start.1 = (bf16[2,256,1280]{1,2,0:T(8,128)(2,1)}, bf16[2,256,1280]{1,2,0:T(8,128)(2,1)}, u32[]{:S(2)}, u32[]{:S(2)}) collective-permute-start(bf16[2,256,1280]{1,2,0:T(8,128)(2,1)} %pad_maximum_fusion), channel_id=1, source_target_pairs={{0,2},{2,4},{4,6},{6,8},{8,10},{10,12},{12,14},{1,3},{3,5},{5,7},{... | collective-permute-start | bytes 3932168 | tf_op jit(solution)/shard_map/ppermute | solution.py:15
  15.4 57.2 %collective-permute-start = (bf16[2,256,1280]{1,2,0:T(8,128)(2,1)}, bf16[2,256,1280]{1,2,0:T(8,128)(2,1)}, u32[]{:S(2)}, u32[]{:S(2)}) collective-permute-start(bf16[2,256,1280]{1,2,0:T(8,128)(2,1)} %pad_maximum_fusion), channel_id=1, source_target_pairs={{2,0},{4,2},{6,4},{8,6},{10,8},{12,10},{14,12},{3,1},{5,3},{7,5},{... | collective-permute-start | bytes 3932168 | tf_op jit(solution)/shard_map/ppermute | solution.py:15
  84.0 55.9 %collective-permute-start.4 = (bf16[2,256,10,128]{3,1,2,0:T(8,128)(2,1)S(1)}, bf16[2,256,10,128]{3,1,2,0:T(8,128)(2,1)}, u32[]{:S(2)}, u32[]{:S(2)}) collective-permute-start(bf16[2,256,10,128]{3,1,2,0:T(8,128)(2,1)S(1)} %pad_maximum_fusion.2), channel_id=1, source_target_pairs={{0,2},{2,4},{4,6},{6,8},{8,10},{10,12},{12,14},{1,3},{3,5},{5,7},{... | collective-permute-start | bytes 3932168 | tf_op jit(solution)/shard_map/ppermute | solution.py:15
  91.2 48.7 %collective-permute-start.5 = (bf16[2,256,10,128]{3,1,2,0:T(8,128)(2,1)}, bf16[2,256,10,128]{3,1,2,0:T(8,128)(2,1)}, u32[]{:S(2)}, u32[]{:S(2)}) collective-permute-start(bf16[2,256,10,128]{3,1,2,0:T(8,128)(2,1)} %pad_maximum_fusion.3), channel_id=1, source_target_pairs={{2,0},{4,2},{6,4},{8,6},{10,8},{12,10},{14,12},{3,1},{5,3},{7,5},{... | collective-permute-start | bytes 3932168 | tf_op jit(solution)/shard_map/ppermute | solution.py:15
  94.1 45.7 %collective-permute-start.6 = (bf16[2,256,10,128]{3,1,2,0:T(8,128)(2,1)}, bf16[2,256,10,128]{3,1,2,0:T(8,128)(2,1)}, u32[]{:S(2)}, u32[]{:S(2)}) collective-permute-start(bf16[2,256,10,128]{3,1,2,0:T(8,128)(2,1)} %pad_maximum_fusion.4), channel_id=1, source_target_pairs={{0,4},{2,6},{4,8},{6,10},{8,12},{10,14},{1,5},{3,7},{5,9},{7,11},{... | collective-permute-start | bytes 3932168 | tf_op jit(solution)/shard_map/ppermute | solution.py:15
  103.2 48.4 %collective-permute-start.7 = (bf16[2,256,10,128]{3,1,2,0:T(8,128)(2,1)}, bf16[2,256,10,128]{3,1,2,0:T(8,128)(2,1)}, u32[]{:S(2)}, u32[]{:S(2)}) collective-permute-start(bf16[2,256,10,128]{3,1,2,0:T(8,128)(2,1)} %pad_maximum_fusion.5), channel_id=1, source_target_pairs={{4,0},{6,2},{8,4},{10,6},{12,8},{14,10},{5,1},{7,3},{9,5},{11,7},{... | collective-permute-start | bytes 3932168 | tf_op jit(solution)/shard_map/ppermute | solution.py:15
where the time goes:
time: 158 us
  waiting for transfers between devices  88.4 us (56%)
  starting transfers between devices  28.5 us (18%)
  matrix products  16 us (10%)
  local copies, waits for them, and re-layouts  12.1 us (8%)
  other arithmetic  8.64 us (5%)
  between operations  4.32 us (3%)
    ppermute x8, waiting for transfers between devices, shifted(): return lax.ppermute(value, axis, pairs)  88.4 us
    ppermute x8, starting transfers between devices, shifted(): return lax.ppermute(value, axis, pairs)  28.5 us
    unnamed x15, local copies, waits for them, and re-layouts  5.35 us
    slice x3, local copies, waits for them, and re-layouts, shards(): remote[0].reshape(head_shape)  4.11 us
    another operation x5, other arithmetic, backward_terms(): results.append(jnp.stack([key_term, value_term]))  3.9 us
    dot_general x5, matrix products, scores_of(): jnp.einsum('qhd,khd->hqk', query_heads, key_heads, preferred_element_type...  3.68 us
    another operation x1, other arithmetic  3.55 us
  transfers between devices with their start and end apart: 8, of which 5 were waited for; matrix products, arithmetic and copies ran while one was open for 10% of the time, Pallas kernels for 0%

commit v1 on v0

v1 whole, which is shorter than its diff:
```python
import functools
import math

import jax
import jax.numpy as jnp
from jax import lax
from jax.experimental import pallas as pl
from jax.experimental.pallas import tpu as pltpu
from jax.sharding import PartitionSpec as P

HDIM = 128
SLOT_OF_OFFSET = {0: 0, 1: 1, -1: 2, 2: 3, -2: 4}
NT = (((1,), (1,)), ((), ()))
TN = (((0,), (0,)), ((), ()))
MESH = pl.DeviceIdType.MESH


def dot(a, b, dims=(((1,), (0,)), ((), ()))):
    return lax.dot_general(a, b, dims, preferred_element_type=jnp.float32)


def kernel(
    half,
    pairs,
    mask_ref,
    q_ref,
    k_ref,
    v_ref,
    g_ref,
    dq_ref,
    dk_ref,
    dv_ref,
    kv,
    qg,
    ret,
    got,
    acc,
    dqs,
    fin,
    wbuf,
    dpbuf,
    x_send,
    x_recv,
    z_send,
    z_recv,
    r_send,
    r_recv,
    o_send,
    o_recv,
):
    tm = lax.axis_index("tm")
    par = lax.rem(tm, 2)
    pair = lax.div(tm, 2)
    other = 1 - par
    partner = tm + 1 - 2 * par
    has_left = pair > 0
    has_right = pair < pairs - 1
    sides = ((0, has_left, tm - 2), (1, has_right, tm + 2))
    scale = HDIM**-0.5

    def cols(which, c):
        return pl.ds(pl.multiple_of((which * half + c) * HDIM, HDIM), HDIM)

    def remote(src, dst, send, recv, to):
        return pltpu.make_async_remote_copy(
            src_ref=src,
            dst_ref=dst,
            send_sem=send,
            recv_sem=recv,
            device_id={"tm": to},
            device_id_type=MESH,
        )

    def x_copy(c, n, frame):
        src = (k_ref, v_ref, q_ref, g_ref)[n].at[:, cols(other, c)]
        dst = kv.at[c, 2 + frame, n] if n < 2 else qg.at[c, frame, n - 2]
        return remote(src, dst, x_send.at[c, n], x_recv.at[c, n], partner)

    def z_copy(c, side, frame, to):
        return remote(
            kv.at[c, 2 + frame],
            kv.at[c, 4 * (1 - side) + frame],
            z_send.at[c, side, frame],
            z_recv.at[c, 1 - side, frame],
            to,
        )

    def z_arrival(c, side, frame):
        return remote(
            kv.at[c, 2 + frame],
            kv.at[c, 4 * side + frame],
            z_send.at[c, side, frame],
            z_recv.at[c, side, frame],
            partner,
        )

    def r_copy(c, side, to):
        return remote(
            ret.at[c, side],
            got.at[c, 1 - side],
            r_send.at[c, side],
            r_recv.at[c, 1 - side],
            to,
        )

    def r_arrival(c, side):
        return remote(
            ret.at[c, side], got.at[c, side], r_send.at[c, side], r_recv.at[c, side], partner
        )

    def o_copy(c, n, which):
        src = dqs.at[c, other] if n == 0 else fin.at[c, n - 1]
        dst = (dq_ref, dk_ref, dv_ref)[n].at[:, cols(which, c)]
        return remote(src, dst, o_send.at[c, n], o_recv.at[c, n], partner)

    barrier = pltpu.get_barrier_semaphore()
    pl.semaphore_signal(barrier, inc=1, device_id={"tm": partner}, device_id_type=MESH)
    for _, there, to in sides:

        @pl.when(there)
        def _():
            pl.semaphore_signal(barrier, inc=1, device_id={"tm": to}, device_id_type=MESH)

    def stage(c, carry):
        here = cols(par, c)
        kv[c, 2 + par, 0] = k_ref[:, here]
        kv[c, 2 + par, 1] = v_ref[:, here]
        qg[c, par, 0] = q_ref[:, here]
        qg[c, par, 1] = g_ref[:, here]
        return carry

    lax.fori_loop(0, half, stage, 0)

    for side, there, _ in sides:

        @pl.when(jnp.logical_not(there))
        def _():
            def clear(c, carry):
                kv[c, pl.ds(4 * side, 2)] = jnp.zeros((2,) + kv.shape[2:], kv.dtype)
                got[c, side] = jnp.zeros(got.shape[2:], got.dtype)
                return carry

            lax.fori_loop(0, half, clear, 0)

    pl.semaphore_wait(barrier, 1 + has_left.astype(jnp.int32) + has_right.astype(jnp.int32))

    def launch(c, carry):
        for n in range(4):
            x_copy(c, n, par).start()
        for side, there, to in sides:

            @pl.when(there)
            def _():
                z_copy(c, side, par, to).start()

        return carry

    lax.fori_loop(0, half, launch, 0)

    def forward(c):
        for n in range(2):
            x_copy(c, n, other).wait_recv()
        for side, there, to in sides:

            @pl.when(there)
            def _():
                z_copy(c, side, other, to).start()

    def compute(c):
        sums = []
        for f in range(2):
            q = qg[c, f, 0]
            g = qg[c, f, 1]
            total = jnp.zeros((1, q.shape[0]), jnp.float32)
            mixed = jnp.zeros((1, q.shape[0]), jnp.float32)
            for j in range(5):
                live = mask_ref[2 * pair + f, SLOT_OF_OFFSET[j - 2]].astype(jnp.float32)
                w = jnp.exp2(dot(kv[c, f + j, 0], q, NT) * (scale * math.log2(math.e))) * live
                dp = dot(kv[c, f + j, 1], g, NT)
                wbuf[f, j] = w
                dpbuf[f, j] = dp
                total = total + jnp.sum(w, axis=0, keepdims=True)
                mixed = mixed + jnp.sum(w * dp, axis=0, keepdims=True)
            inverse = 1.0 / total
            sums.append((inverse, mixed * inverse))
        dq = [None, None]
        for slot in range(6):
            dk = dv = None
            for f in range(2):
                j = slot - f
                if not 0 <= j < 5:
                    continue
                inverse, delta = sums[f]
                p = wbuf[f, j] * inverse
                ds = (p * (dpbuf[f, j] - delta)).astype(jnp.bfloat16)
                dv_term = dot(p.astype(jnp.bfloat16), qg[c, f, 1])
                dk_term = dot(ds, qg[c, f, 0])
                dq_term = dot(ds, kv[c, slot, 0], TN)
                dv = dv_term if dv is None else dv + dv_term
                dk = dk_term if dk is None else dk + dk_term
                dq[f] = dq_term if dq[f] is None else dq[f] + dq_term
            dk = dk * scale
            if 2 <= slot < 4:
                acc[c, slot - 2, 0] = dk
                acc[c, slot - 2, 1] = dv
            else:
                ret[c, slot // 4, slot % 2, 0] = dk.astype(jnp.bfloat16)
                ret[c, slot // 4, slot % 2, 1] = dv.astype(jnp.bfloat16)
        for f in range(2):
            dqs[c, f] = (dq[f] * scale).astype(jnp.bfloat16)

    def finish(c):
        for side, there, _ in sides:

            @pl.when(there)
            def _():
                r_arrival(c, side).wait_recv()

        def summed(frame, n):
            total = acc[c, frame, n]
            for side in range(2):
                total = total + got[c, side, frame, n].astype(jnp.float32)
            return total.astype(jnp.bfloat16)

        for n in range(2):
            fin[c, n] = summed(other, n)
            o_copy(c, n + 1, par).start()
        for n in range(2):
            (dk_ref, dv_ref)[n][:, cols(par, c)] = summed(par, n)

    ahead = min(2, half)
    for c in range(ahead):
        forward(c)

    def step(c, carry):
        @pl.when(c + ahead < half)
        def _():
            forward(c + ahead)

        for n in range(2, 4):
            x_copy(c, n, other).wait_recv()
        for side, there, _ in sides:

            @pl.when(there)
            def _():
                for frame in range(2):
                    z_arrival(c, side, frame).wait_recv()

        compute(c)
        for side, there, to in sides:

            @pl.when(there)
            def _():
                r_copy(c, side, to).start()

        o_copy(c, 0, par).start()
        dq_ref[:, cols(par, c)] = dqs[c, par]

        @pl.when(c >= 1)
        def _():
            finish(c - 1)

        return carry

    lax.fori_loop(0, half, step, 0)
    finish(half - 1)

    def drain(c, carry):
        for n in range(4):
            x_copy(c, n, par).wait_send()
        for side, there, to in sides:

            @pl.when(there)
            def _():
                for frame in range(2):
                    z_copy(c, side, frame, to).wait_send()
                r_copy(c, side, to).wait_send()

        for n in range(3):
            o_copy(c, n, par).wait_send()
            o_copy(c, n, other).wait_recv()
        return carry

    lax.fori_loop(0, half, drain, 0)


def shards(queries, keys, values, out_grad, pair_mask):
    rows, width = queries.shape
    half = width // HDIM // 2
    pairs = lax.axis_size("tm") // 2
    low, full = jnp.bfloat16, jnp.float32
    dma = pltpu.SemaphoreType.DMA
    flops = 2 * rows * rows * HDIM * 5 * 10 * half
    out = jax.ShapeDtypeStruct((rows, width), low)
    vmem = pl.BlockSpec(memory_space=pltpu.VMEM)
    return pl.pallas_call(
        functools.partial(kernel, half, pairs),
        out_shape=(out, out, out),
        in_specs=[pl.BlockSpec(memory_space=pltpu.SMEM)] + [vmem] * 4,
        out_specs=(vmem, vmem, vmem),
        scratch_shapes=[
            pltpu.VMEM((half, 6, 2, rows, HDIM), low),
            pltpu.VMEM((half, 2, 2, rows, HDIM), low),
            pltpu.VMEM((half, 2, 2, 2, rows, HDIM), low),
            pltpu.VMEM((half, 2, 2, 2, rows, HDIM), low),
            pltpu.VMEM((half, 2, 2, rows, HDIM), full),
            pltpu.VMEM((half, 2, rows, HDIM), low),
            pltpu.VMEM((half, 2, rows, HDIM), low),
            pltpu.VMEM((2, 5, rows, rows), full),
            pltpu.VMEM((2, 5, rows, rows), full),
            dma((half, 4)),
            dma((half, 4)),
            dma((half, 2, 2)),
            dma((half, 2, 2)),
            dma((half, 2)),
            dma((half, 2)),
            dma((half, 3)),
            dma((half, 3)),
        ],
        cost_estimate=pl.CostEstimate(
            flops=flops, bytes_accessed=14 * rows * width, transcendentals=10 * half * rows * rows
        ),
        compiler_params=pltpu.CompilerParams(
            collective_id=0, has_side_effects=True, vmem_limit_bytes=48 * 1024 * 1024
        ),
    )(pair_mask, queries, keys, values, out_grad)


def solution(mesh):
    split = P(("groups", "tm"), "head")
    return jax.shard_map(
        shards,
        mesh=mesh,
        in_specs=(split, split, split, split, P("groups", None)),
        out_specs=(split, split, split),
        check_vma=False,
    )
```

time: 158 us -> 75.9 us (0.48)
  waiting for transfers between devices: 88.4 us -> 0 us
  Pallas kernels: 0 us -> 67.4 us
  starting transfers between devices: 28.5 us -> 0 us
  matrix products: 16 us -> 0 us
  other arithmetic: 8.64 us -> 0 us
  local copies, waits for them, and re-layouts: 12.1 us -> 7.54 us
  between operations: 4.32 us -> 0.65 us
    ppermute x8 -> x0, waiting for transfers between devices: 88.4 us -> none  [shifted(): return lax.ppermute(value, axis, pairs)]
    pallas_call x0 -> x1, Pallas kernels: none -> 67.4 us  [shards(): pl.pallas_call(functools.partial(kernel, half, pairs), out_shape=(out, ou...]
    ppermute x8 -> x0, starting transfers between devices: 28.5 us -> none  [shifted(): return lax.ppermute(value, axis, pairs)]
    dot_general x30 -> x0, matrix products: 16 us -> none  [the longest x5 3.68 us: scores_of(): jnp.einsum('qhd,khd->hqk', query_heads, key_heads, preferred_element_type...]
    another operation x7 -> x0, other arithmetic: 8.63 us -> none  [the longest x5 3.9 us: backward_terms(): results.append(jnp.stack([key_term, value_term]))]
    slice x7 -> x0, local copies, waits for them, and re-layouts: 6.06 us -> none  [the longest x3 4.11 us: shards(): remote[0].reshape(head_shape)]
    unnamed x15 -> x13, local copies, waits for them, and re-layouts: 5.35 us -> 7.54 us
  transfers between devices with their start and end apart: 8 -> 0, of which waited for: 5 -> 0; matrix products, arithmetic and copies ran while one was open for 10% -> 0% of each run, Pallas kernels for 0% -> 0%
where the time goes in v1:
time: 75.9 us; the launch traced here: 75.6 us
  Pallas kernels  67.4 us (89%)
  local copies, waits for them, and re-layouts  7.54 us (10%)
    pallas_call x1, Pallas kernels, shards(): pl.pallas_call(functools.partial(kernel, half, pairs), out_shape=(out, ou...  67.4 us
    unnamed x13, local copies, waits for them, and re-layouts  7.54 us

profile of v1, /device:TPU:0, one launch (start us, length us, event | category | flops | bytes accessed | tf_op | source)
XLA Modules:
  0.0 75.6 jit_solution(7529370791850811536)
XLA Ops:
  0.6 0.0 copy-start
  0.6 1.1 %copy-done = bf16[256,1280]{1,0:T(8,128)(2,1)S(1)} copy-done((bf16[256,1280]{1,0:T(8,128)(2,1)S(1)}, bf16[256,1280]{1,0:T(8,128)(2,1)}, u32[]{:S(2)}) %copy-start) | copy-done | bytes 655384
  1.7 0.0 copy-start.1
  1.7 1.1 %copy-done.1 = bf16[256,1280]{1,0:T(8,128)(2,1)S(1)} copy-done((bf16[256,1280]{1,0:T(8,128)(2,1)S(1)}, bf16[256,1280]{1,0:T(8,128)(2,1)}, u32[]{:S(2)}) %copy-start.1) | copy-done | bytes 655384
  2.8 0.0 copy-start.2
  2.8 1.1 %copy-done.2 = bf16[256,1280]{1,0:T(8,128)(2,1)S(1)} copy-done((bf16[256,1280]{1,0:T(8,128)(2,1)S(1)}, bf16[256,1280]{1,0:T(8,128)(2,1)}, u32[]{:S(2)}) %copy-start.2) | copy-done | bytes 655384
  3.9 0.0 copy-start.3
  3.9 1.1 %copy-done.3 = bf16[256,1280]{1,0:T(8,128)(2,1)S(1)} copy-done((bf16[256,1280]{1,0:T(8,128)(2,1)S(1)}, bf16[256,1280]{1,0:T(8,128)(2,1)}, u32[]{:S(2)}) %copy-start.3) | copy-done | bytes 655384
  5.0 0.0 copy-start.4
  5.0 0.7 copy-done.4
  5.7 67.4 %shard_map.76 = (bf16[256,1280]{1,0:T(8,128)(2,1)S(1)}, bf16[256,1280]{1,0:T(8,128)(2,1)S(1)}, bf16[256,1280]{1,0:T(8,128)(2,1)S(1)}) custom-call(s32[8,5]{1,0:T(8,128)S(1)} %copy-done.4, bf16[256,1280]{1,0:T(8,128)(2,1)S(1)} %copy-done, bf16[256,1280]{1,0:T(8,128)(2,1)S(1)} %copy-done.1, bf16[256,1280]{1,0:T(8,128)(2,1)S(1)} %copy-done.2, ...), custom_call_target="tpu_custom_call" | custom-call | flops 4194304000 | bytes 4587520 | tf_op jit(solution)/shard_map/pallas_call | solution.py:296
  73.1 0.8 %copy.11 = bf16[256,1280]{1,0:T(8,128)(2,1)} copy(bf16[256,1280]{1,0:T(8,128)(2,1)S(1)} %get-tuple-element.6) | data formatting | bytes 1310720
  73.9 0.8 %copy.12 = bf16[256,1280]{1,0:T(8,128)(2,1)} copy(bf16[256,1280]{1,0:T(8,128)(2,1)S(1)} %get-tuple-element.7) | data formatting | bytes 1310720
  74.8 0.8 %copy.13 = bf16[256,1280]{1,0:T(8,128)(2,1)} copy(bf16[256,1280]{1,0:T(8,128)(2,1)S(1)} %get-tuple-element.8) | data formatting | bytes 1310720
Async XLA Ops:
  0.6 1.1 %copy-start = (bf16[256,1280]{1,0:T(8,128)(2,1)S(1)}, bf16[256,1280]{1,0:T(8,128)(2,1)}, u32[]{:S(2)}) copy-start(bf16[256,1280]{1,0:T(8,128)(2,1)} %q_ref.1) | copy-start | bytes 1966084
  1.7 1.1 %copy-start.1 = (bf16[256,1280]{1,0:T(8,128)(2,1)S(1)}, bf16[256,1280]{1,0:T(8,128)(2,1)}, u32[]{:S(2)}) copy-start(bf16[256,1280]{1,0:T(8,128)(2,1)} %k_ref.1) | copy-start | bytes 1966084
  2.8 1.1 %copy-start.2 = (bf16[256,1280]{1,0:T(8,128)(2,1)S(1)}, bf16[256,1280]{1,0:T(8,128)(2,1)}, u32[]{:S(2)}) copy-start(bf16[256,1280]{1,0:T(8,128)(2,1)} %v_ref.1) | copy-start | bytes 1966084
  3.9 1.1 %copy-start.3 = (bf16[256,1280]{1,0:T(8,128)(2,1)S(1)}, bf16[256,1280]{1,0:T(8,128)(2,1)}, u32[]{:S(2)}) copy-start(bf16[256,1280]{1,0:T(8,128)(2,1)} %g_ref.1) | copy-start | bytes 1966084
  5.0 0.7 copy-start.4

commit v2 on v1

--- a/solution.py
+++ b/solution.py
@@ -39,6 +39,7 @@
     fin,
     wbuf,
     dpbuf,
+    local,
     x_send,
     x_recv,
     z_send,
@@ -121,12 +122,14 @@
         def _():
             pl.semaphore_signal(barrier, inc=1, device_id={"tm": to}, device_id_type=MESH)
 
+    def own_copy(c, n):
+        src = (k_ref, v_ref, q_ref, g_ref)[n].at[:, cols(par, c)]
+        dst = kv.at[c, 2 + par, n] if n < 2 else qg.at[c, par, n - 2]
+        return pltpu.make_async_copy(src, dst, local.at[c, n])
+
     def stage(c, carry):
-        here = cols(par, c)
-        kv[c, 2 + par, 0] = k_ref[:, here]
-        kv[c, 2 + par, 1] = v_ref[:, here]
-        qg[c, par, 0] = q_ref[:, here]
-        qg[c, par, 1] = g_ref[:, here]
+        for n in range(4):
+            own_copy(c, n).start()
         return carry
 
     lax.fori_loop(0, half, stage, 0)
@@ -147,6 +150,8 @@
     def launch(c, carry):
         for n in range(4):
             x_copy(c, n, par).start()
+        for n in range(2):
+            own_copy(c, n).wait()
         for side, there, to in sides:
 
             @pl.when(there)
@@ -239,6 +244,7 @@
 
         for n in range(2, 4):
             x_copy(c, n, other).wait_recv()
+            own_copy(c, n).wait()
         for side, there, _ in sides:
 
             @pl.when(there)
@@ -296,7 +302,7 @@
     return pl.pallas_call(
         functools.partial(kernel, half, pairs),
         out_shape=(out, out, out),
-        in_specs=[pl.BlockSpec(memory_space=pltpu.SMEM)] + [vmem] * 4,
+        in_specs=[pl.BlockSpec(memory_space=pltpu.SMEM)] + [pl.BlockSpec(memory_space=pl.ANY)] * 4,
         out_specs=(vmem, vmem, vmem),
         scratch_shapes=[
             pltpu.VMEM((half, 6, 2, rows, HDIM), low),
@@ -310,6 +316,7 @@
             pltpu.VMEM((2, 5, rows, rows), full),
             dma((half, 4)),
             dma((half, 4)),
+            dma((half, 4)),
             dma((half, 2, 2)),
             dma((half, 2, 2)),
             dma((half, 2)),
@@ -321,7 +328,7 @@
             flops=flops, bytes_accessed=14 * rows * width, transcendentals=10 * half * rows * rows
         ),
         compiler_params=pltpu.CompilerParams(
-            collective_id=0, has_side_effects=True, vmem_limit_bytes=48 * 1024 * 1024
+            collective_id=0, has_side_effects=True, vmem_limit_bytes=60 * 1024 * 1024
         ),
     )(pair_mask, queries, keys, values, out_grad)
 

time: 75.9 us -> 74.1 us (0.976)
  local copies, waits for them, and re-layouts: 7.54 us -> 4.19 us
  Pallas kernels: 67.4 us -> 69 us
    unnamed x13 -> x7, local copies, waits for them, and re-layouts: 7.54 us -> 4.19 us
    pallas_call x1, Pallas kernels: 67.4 us -> 69 us  [shards(): pl.pallas_call(functools.partial(kernel, half, pairs), out_shape=(out, ou...]
where the time goes in v2:
time: 74.1 us; the launch traced here: 73.9 us
  Pallas kernels  69 us (93%)
  local copies, waits for them, and re-layouts  4.19 us (6%)
    pallas_call x1, Pallas kernels, shards(): pl.pallas_call(functools.partial(kernel, half, pairs), out_shape=(out, ou...  69 us
    unnamed x7, local copies, waits for them, and re-layouts  4.19 us

profile of v2, /device:TPU:0, one launch (start us, length us, event | category | flops | bytes accessed | tf_op | source)
XLA Modules:
  0.0 73.9 jit_solution(11690457557371368736)
XLA Ops:
  0.6 69.0 %shard_map.76 = (bf16[256,1280]{1,0:T(8,128)(2,1)}, bf16[256,1280]{1,0:T(8,128)(2,1)}, bf16[256,1280]{1,0:T(8,128)(2,1)}) custom-call(s32[8,5]{1,0:T(8,128)} %mask_ref.1, bf16[256,1280]{1,0:T(8,128)(2,1)} %q_ref.1, bf16[256,1280]{1,0:T(8,128)(2,1)} %k_ref.1, bf16[256,1280]{1,0:T(8,128)(2,1)} %v_ref.1, bf16[256,1280]{1,0:T(8,128)(2,1)} %g_ref.1), custom_call_target="tpu_custom_call" | custom-call | flops 4194304000 | bytes 4587520 | tf_op jit(solution)/shard_map/pallas_call | solution.py:302
  69.7 0.0 copy-start.1
  69.7 2.0 %copy.11 = bf16[256,1280]{1,0:T(8,128)(2,1)} copy(bf16[256,1280]{1,0:T(8,128)(2,1)} %get-tuple-element.6) | data formatting | bytes 1310720
  71.7 0.0 copy-done.1
  71.7 0.0 copy-start
  71.7 0.8 %copy.12 = bf16[256,1280]{1,0:T(8,128)(2,1)} copy(bf16[256,1280]{1,0:T(8,128)(2,1)S(1)} %copy-done.1) | data formatting | bytes 1310720
  72.6 0.5 copy-done
  73.1 0.8 %copy.13 = bf16[256,1280]{1,0:T(8,128)(2,1)} copy(bf16[256,1280]{1,0:T(8,128)(2,1)S(1)} %copy-done) | data formatting | bytes 1310720
Async XLA Ops:
  69.7 2.0 %copy-start.1 = (bf16[256,1280]{1,0:T(8,128)(2,1)S(1)}, bf16[256,1280]{1,0:T(8,128)(2,1)}, u32[]{:S(2)}) copy-start(bf16[256,1280]{1,0:T(8,128)(2,1)} %get-tuple-element.7) | copy-start | bytes 1966084
  71.7 1.3 %copy-start = (bf16[256,1280]{1,0:T(8,128)(2,1)S(1)}, bf16[256,1280]{1,0:T(8,128)(2,1)}, u32[]{:S(2)}) copy-start(bf16[256,1280]{1,0:T(8,128)(2,1)} %get-tuple-element.8) | copy-start | bytes 1966084

commit v3 on v2

v3 whole, which is shorter than its diff:
```python
import functools
import math

import jax
import jax.numpy as jnp
from jax import lax
from jax.experimental import pallas as pl
from jax.experimental.pallas import tpu as pltpu
from jax.sharding import PartitionSpec as P

HDIM = 128
SLOT_OF_OFFSET = {0: 0, 1: 1, -1: 2, 2: 3, -2: 4}
NT = (((1,), (1,)), ((), ()))
TN = (((0,), (0,)), ((), ()))
MESH = pl.DeviceIdType.MESH


def dot(a, b, dims=(((1,), (0,)), ((), ()))):
    return lax.dot_general(a, b, dims, preferred_element_type=jnp.float32)


def kernel(
    half,
    pairs,
    mask_ref,
    q_ref,
    k_ref,
    v_ref,
    g_ref,
    dq_ref,
    dk_ref,
    dv_ref,
    near,
    kv,
    ret,
    got,
    acc,
    kvs,
    fin,
    own_part,
    part,
    part_in,
    stat,
    stat_in,
    wbuf,
    dpbuf,
    local,
    x_send,
    x_recv,
    z_send,
    z_recv,
    r_send,
    r_recv,
    p_send,
    p_recv,
    s_send,
    s_recv,
    o_send,
    o_recv,
):
    tm = lax.axis_index("tm")
    par = lax.rem(tm, 2)
    pair = lax.div(tm, 2)
    other = 1 - par
    partner = tm + 1 - 2 * par
    has_left = pair > 0
    has_right = pair < pairs - 1
    sides = ((0, has_left, tm - 2), (1, has_right, tm + 2))
    scale = HDIM**-0.5

    def cols(which, c):
        return pl.ds(pl.multiple_of((which * half + c) * HDIM, HDIM), HDIM)

    def remote(src, dst, send, recv, to):
        return pltpu.make_async_remote_copy(
            src_ref=src,
            dst_ref=dst,
            send_sem=send,
            recv_sem=recv,
            device_id={"tm": to},
            device_id_type=MESH,
        )

    sources = (q_ref, g_ref, k_ref, v_ref)

    def place(c, n, frame):
        return near.at[c, 2 + frame, n] if n < 2 else kv.at[c, frame, n - 2]

    def x_copy(c, n, frame):
        src = sources[n].at[:, cols(other, c)]
        return remote(src, place(c, n, frame), x_send.at[c, n], x_recv.at[c, n], partner)

    def z_copy(c, side, frame, to):
        return remote(
            near.at[c, 2 + frame],
            near.at[c, 4 * (1 - side) + frame],
            z_send.at[c, side, frame],
            z_recv.at[c, 1 - side, frame],
            to,
        )

    def z_arrival(c, side, frame):
        return remote(
            near.at[c, 2 + frame],
            near.at[c, 4 * side + frame],
            z_send.at[c, side, frame],
            z_recv.at[c, side, frame],
            partner,
        )

    def swap(src, dst, send, recv, c, side, to):
        return remote(
            src, dst.at[c, 1 - side], send.at[c, side], recv.at[c, 1 - side], to
        )

    def r_copy(c, side, to):
        return swap(ret.at[c, side], got, r_send, r_recv, c, side, to)

    def p_copy(c, side, to):
        return swap(part.at[c, side], part_in, p_send, p_recv, c, side, to)

    def s_copy(c, side, to):
        return swap(stat.at[c], stat_in, s_send, s_recv, c, side, to)

    def r_arrival(c, side):
        return remote(
            ret.at[c, side], got.at[c, side], r_send.at[c, side], r_recv.at[c, side], partner
        )

    def p_arrival(c, side):
        return remote(
            part.at[c, side], part_in.at[c, side], p_send.at[c, side], p_recv.at[c, side], partner
        )

    def s_arrival(c, side):
        return remote(
            stat.at[c], stat_in.at[c, side], s_send.at[c, side], s_recv.at[c, side], partner
        )

    def o_copy(c, n, which):
        src = fin.at[c] if n == 0 else kvs.at[c, other, n - 1]
        dst = (dq_ref, dk_ref, dv_ref)[n].at[:, cols(which, c)]
        return remote(src, dst, o_send.at[c, n], o_recv.at[c, n], partner)

    def each_side(act):
        for side, there, to in sides:

            @pl.when(there)
            def _():
                act(side, to)

    barrier = pltpu.get_barrier_semaphore()
    pl.semaphore_signal(barrier, inc=1, device_id={"tm": partner}, device_id_type=MESH)
    for _, there, to in sides:

        @pl.when(there)
        def _():
            pl.semaphore_signal(barrier, inc=1, device_id={"tm": to}, device_id_type=MESH)

    def own_copy(c, n):
        src = sources[n].at[:, cols(par, c)]
        return pltpu.make_async_copy(src, place(c, n, par), local.at[c, n])

    def stage(c, carry):
        for n in range(4):
            own_copy(c, n).start()
        return carry

    lax.fori_loop(0, half, stage, 0)

    for side, there, _ in sides:

        @pl.when(jnp.logical_not(there))
        def _():
            def clear(c, carry):
                near[c, pl.ds(4 * side, 2)] = jnp.zeros((2,) + near.shape[2:], near.dtype)
                got[c, side] = jnp.zeros(got.shape[2:], got.dtype)
                part_in[c, side] = jnp.zeros(part_in.shape[2:], part_in.dtype)
                stat_in[c, side] = jnp.zeros(stat_in.shape[2:], stat_in.dtype)
                return carry

            lax.fori_loop(0, half, clear, 0)

    pl.semaphore_wait(barrier, 1 + has_left.astype(jnp.int32) + has_right.astype(jnp.int32))

    def launch(c, carry):
        for n in range(4):
            x_copy(c, n, par).start()
        return carry

    lax.fori_loop(0, half, launch, 0)

    def send_own(c):
        for n in range(2):
            own_copy(c, n).wait()
        each_side(lambda side, to: z_copy(c, side, par, to).start())

    ahead = min(2, half)

    def forward(c):
        for n in range(2):
            x_copy(c, n, other).wait_recv()
        each_side(lambda side, to: z_copy(c, side, other, to).start())

        @pl.when(c + ahead < half)
        def _():
            send_own(c + ahead)

    for c in range(ahead):
        send_own(c)

    def first(c):
        now = lax.rem(c, 2)
        for slot in range(6):
            q = near[c, slot, 0]
            g = near[c, slot, 1]
            frame = lax.rem(2 * pair + 2 * pairs - 2 + slot, 2 * pairs)
            total = jnp.zeros((1, q.shape[0]), jnp.float32)
            mixed = jnp.zeros((1, q.shape[0]), jnp.float32)
            for f in range(2):
                j = slot - f
                if not 0 <= j < 5:
                    continue
                live = mask_ref[frame, SLOT_OF_OFFSET[2 - j]].astype(jnp.float32)
                w = jnp.exp2(dot(kv[c, f, 0], q, NT) * (scale * math.log2(math.e))) * live
                dp = dot(kv[c, f, 1], g, NT)
                wbuf[now, f, j] = w
                dpbuf[now, f, j] = dp
                total = total + jnp.sum(w, axis=0, keepdims=True)
                mixed = mixed + jnp.sum(w * dp, axis=0, keepdims=True)
            row = 2 * (slot % 2)
            if 2 <= slot < 4:
                own_part[c, row : row + 1] = total
                own_part[c, row + 1 : row + 2] = mixed
            else:
                part[c, slot // 4, row : row + 1] = total
                part[c, slot // 4, row + 1 : row + 2] = mixed

    def combine(c):
        each_side(lambda side, to: p_arrival(c, side).wait_recv())
        sums = own_part[c] + part_in[c, 0] + part_in[c, 1]
        for row in (0, 2):
            inverse = 1.0 / sums[row : row + 1]
            stat[c, row : row + 1] = inverse
            stat[c, row + 1 : row + 2] = sums[row + 1 : row + 2] * inverse
        each_side(lambda side, to: s_copy(c, side, to).start())

    def second(c):
        now = lax.rem(c, 2)
        each_side(lambda side, to: s_arrival(c, side).wait_recv())
        dk = [None, None]
        dv = [None, None]
        for slot in range(6):
            row = 2 * (slot % 2)
            held = stat[c] if 2 <= slot < 4 else stat_in[c, slot // 4]
            inverse = held[row : row + 1]
            delta = held[row + 1 : row + 2]
            q = near[c, slot, 0]
            g = near[c, slot, 1]
            dq = None
            for f in range(2):
                j = slot - f
                if not 0 <= j < 5:
                    continue
                p = wbuf[now, f, j] * inverse
                ds = (p * (dpbuf[now, f, j] - delta)).astype(jnp.bfloat16)
                dv_term = dot(p.astype(jnp.bfloat16), g)
                dk_term = dot(ds, q)
                dq_term = dot(ds, kv[c, f, 0], TN)
                dv[f] = dv_term if dv[f] is None else dv[f] + dv_term
                dk[f] = dk_term if dk[f] is None else dk[f] + dk_term
                dq = dq_term if dq is None else dq + dq_term
            dq = dq * scale
            if 2 <= slot < 4:
                acc[c, slot - 2] = dq
            else:
                ret[c, slot // 4, slot % 2] = dq.astype(jnp.bfloat16)
        each_side(lambda side, to: r_copy(c, side, to).start())
        for f in range(2):
            kvs[c, f, 0] = (dk[f] * scale).astype(jnp.bfloat16)
            kvs[c, f, 1] = dv[f].astype(jnp.bfloat16)
        for n in range(2):
            o_copy(c, n + 1, par).start()
        for n in range(2):
            (dk_ref, dv_ref)[n][:, cols(par, c)] = kvs[c, par, n]

    def finish(c):
        each_side(lambda side, to: r_arrival(c, side).wait_recv())

        def summed(frame):
            total = acc[c, frame]
            for side in range(2):
                total = total + got[c, side, frame].astype(jnp.float32)
            return total.astype(jnp.bfloat16)

        fin[c] = summed(other)
        o_copy(c, 0, par).start()
        dq_ref[:, cols(par, c)] = summed(par)

    forward(0)

    def step(c, carry):
        @pl.when(jnp.logical_and(c >= 1, c <= half))
        def _():
            combine(c - 1)

        @pl.when(c < half)
        def _():
            for n in range(2, 4):
                x_copy(c, n, other).wait_recv()
                own_copy(c, n).wait()
            for frame in range(2):
                each_side(lambda side, to: z_arrival(c, side, frame).wait_recv())
            first(c)
            each_side(lambda side, to: p_copy(c, side, to).start())

        @pl.when(c + 1 < half)
        def _():
            forward(c + 1)

        @pl.when(jnp.logical_and(c >= 1, c <= half))
        def _():
            second(c - 1)

        @pl.when(c >= 2)
        def _():
            finish(c - 2)

        return carry

    lax.fori_loop(0, half + 2, step, 0)

    def drain(c, carry):
        for n in range(4):
            x_copy(c, n, par).wait_send()

        def sent(side, to):
            for frame in range(2):
                z_copy(c, side, frame, to).wait_send()
            for copy in (r_copy, p_copy, s_copy):
                copy(c, side, to).wait_send()

        each_side(sent)
        for n in range(3):
            o_copy(c, n, par).wait_send()
            o_copy(c, n, other).wait_recv()
        return carry

    lax.fori_loop(0, half, drain, 0)


def shards(queries, keys, values, out_grad, pair_mask):
    rows, width = queries.shape
    half = width // HDIM // 2
    pairs = lax.axis_size("tm") // 2
    low, full = jnp.bfloat16, jnp.float32
    dma = pltpu.SemaphoreType.DMA
    flops = 2 * rows * rows * HDIM * 5 * 10 * half
    out = jax.ShapeDtypeStruct((rows, width), low)
    vmem = pl.BlockSpec(memory_space=pltpu.VMEM)
    return pl.pallas_call(
        functools.partial(kernel, half, pairs),
        out_shape=(out, out, out),
        in_specs=[pl.BlockSpec(memory_space=pltpu.SMEM)] + [pl.BlockSpec(memory_space=pl.ANY)] * 4,
        out_specs=(vmem, vmem, vmem),
        scratch_shapes=[
            pltpu.VMEM((half, 6, 2, rows, HDIM), low),
            pltpu.VMEM((half, 2, 2, rows, HDIM), low),
            pltpu.VMEM((half, 2, 2, rows, HDIM), low),
            pltpu.VMEM((half, 2, 2, rows, HDIM), low),
            pltpu.VMEM((half, 2, rows, HDIM), full),
            pltpu.VMEM((half, 2, 2, rows, HDIM), low),
            pltpu.VMEM((half, rows, HDIM), low),
            pltpu.VMEM((half, 4, rows), full),
            pltpu.VMEM((half, 2, 4, rows), full),
            pltpu.VMEM((half, 2, 4, rows), full),
            pltpu.VMEM((half, 4, rows), full),
            pltpu.VMEM((half, 2, 4, rows), full),
            pltpu.VMEM((2, 2, 5, rows, rows), full),
            pltpu.VMEM((2, 2, 5, rows, rows), full),
            dma((half, 4)),
            dma((half, 4)),
            dma((half, 4)),
            dma((half, 2, 2)),
            dma((half, 2, 2)),
            dma((half, 2)),
            dma((half, 2)),
            dma((half, 2)),
            dma((half, 2)),
            dma((half, 2)),
            dma((half, 2)),
            dma((half, 3)),
            dma((half, 3)),
        ],
        cost_estimate=pl.CostEstimate(
            flops=flops, bytes_accessed=14 * rows * width, transcendentals=10 * half * rows * rows
        ),
        compiler_params=pltpu.CompilerParams(
            collective_id=0, has_side_effects=True, vmem_limit_bytes=60 * 1024 * 1024
        ),
    )(pair_mask, queries, keys, values, out_grad)


def solution(mesh):
    split = P(("groups", "tm"), "head")
    return jax.shard_map(
        shards,
        mesh=mesh,
        in_specs=(split, split, split, split, P("groups", None)),
        out_specs=(split, split, split),
        check_vma=False,
    )
```

time: 74.1 us -> 67.5 us (0.911)
  Pallas kernels: 69 us -> 62.5 us
    pallas_call x1, Pallas kernels: 69 us -> 62.5 us  [shards(): pl.pallas_call(functools.partial(kernel, half, pairs), out_shape=(out, ou...]
where the time goes in v3:
time: 67.5 us; the launch traced here: 67.3 us
  Pallas kernels  62.5 us (93%)
  local copies, waits for them, and re-layouts  4.19 us (6%)
    pallas_call x1, Pallas kernels, shards(): pl.pallas_call(functools.partial(kernel, half, pairs), out_shape=(out, ou...  62.5 us
    unnamed x7, local copies, waits for them, and re-layouts  4.19 us

profile of v3, /device:TPU:0, one launch (start us, length us, event | category | flops | bytes accessed | tf_op | source)
XLA Modules:
  0.0 67.3 jit_solution(12696526091519629022)
XLA Ops:
  0.6 62.5 %shard_map.76 = (bf16[256,1280]{1,0:T(8,128)(2,1)}, bf16[256,1280]{1,0:T(8,128)(2,1)}, bf16[256,1280]{1,0:T(8,128)(2,1)}) custom-call(s32[8,5]{1,0:T(8,128)} %mask_ref.1, bf16[256,1280]{1,0:T(8,128)(2,1)} %q_ref.1, bf16[256,1280]{1,0:T(8,128)(2,1)} %k_ref.1, bf16[256,1280]{1,0:T(8,128)(2,1)} %v_ref.1, bf16[256,1280]{1,0:T(8,128)(2,1)} %g_ref.1), custom_call_target="tpu_custom_call" | custom-call | flops 4194304000 | bytes 4587520 | tf_op jit(solution)/shard_map/pallas_call | solution.py:361
  63.1 0.0 copy-start.1
  63.1 2.0 %copy.11 = bf16[256,1280]{1,0:T(8,128)(2,1)} copy(bf16[256,1280]{1,0:T(8,128)(2,1)} %get-tuple-element.6) | data formatting | bytes 1310720
  65.1 0.0 copy-done.1
  65.1 0.0 copy-start
  65.2 0.8 %copy.12 = bf16[256,1280]{1,0:T(8,128)(2,1)} copy(bf16[256,1280]{1,0:T(8,128)(2,1)S(1)} %copy-done.1) | data formatting | bytes 1310720
  66.0 0.5 copy-done
  66.5 0.8 %copy.13 = bf16[256,1280]{1,0:T(8,128)(2,1)} copy(bf16[256,1280]{1,0:T(8,128)(2,1)S(1)} %copy-done) | data formatting | bytes 1310720
Async XLA Ops:
  63.1 2.0 %copy-start.1 = (bf16[256,1280]{1,0:T(8,128)(2,1)S(1)}, bf16[256,1280]{1,0:T(8,128)(2,1)}, u32[]{:S(2)}) copy-start(bf16[256,1280]{1,0:T(8,128)(2,1)} %get-tuple-element.7) | copy-start | bytes 1966084
  65.1 1.3 %copy-start = (bf16[256,1280]{1,0:T(8,128)(2,1)S(1)}, bf16[256,1280]{1,0:T(8,128)(2,1)}, u32[]{:S(2)}) copy-start(bf16[256,1280]{1,0:T(8,128)(2,1)} %get-tuple-element.8) | copy-start | bytes 1966084

commit v4 on v3

--- a/solution.py
+++ b/solution.py
@@ -12,6 +12,7 @@
 SLOT_OF_OFFSET = {0: 0, 1: 1, -1: 2, 2: 3, -2: 4}
 NT = (((1,), (1,)), ((), ()))
 TN = (((0,), (0,)), ((), ()))
+PIECES = 2
 MESH = pl.DeviceIdType.MESH
 
 
@@ -37,6 +38,7 @@
     acc,
     kvs,
     fin,
+    mine,
     own_part,
     part,
     part_in,
@@ -44,6 +46,7 @@
     stat_in,
     wbuf,
     dpbuf,
+    keep,
     local,
     x_send,
     x_recv,
@@ -141,6 +144,11 @@
         src = fin.at[c] if n == 0 else kvs.at[c, other, n - 1]
         dst = (dq_ref, dk_ref, dv_ref)[n].at[:, cols(which, c)]
         return remote(src, dst, o_send.at[c, n], o_recv.at[c, n], partner)
+
+    def keep_copy(c, n):
+        src = mine.at[c] if n == 0 else kvs.at[c, par, n - 1]
+        dst = (dq_ref, dk_ref, dv_ref)[n].at[:, cols(par, c)]
+        return pltpu.make_async_copy(src, dst, keep.at[c, n])
 
     def each_side(act):
         for side, there, to in sides:
@@ -282,7 +290,7 @@
         for n in range(2):
             o_copy(c, n + 1, par).start()
         for n in range(2):
-            (dk_ref, dv_ref)[n][:, cols(par, c)] = kvs[c, par, n]
+            keep_copy(c, n + 1).start()
 
     def finish(c):
         each_side(lambda side, to: r_arrival(c, side).wait_recv())
@@ -295,7 +303,8 @@
 
         fin[c] = summed(other)
         o_copy(c, 0, par).start()
-        dq_ref[:, cols(par, c)] = summed(par)
+        mine[c] = summed(par)
+        keep_copy(c, 0).start()
 
     forward(0)
 
@@ -344,9 +353,33 @@
         for n in range(3):
             o_copy(c, n, par).wait_send()
             o_copy(c, n, other).wait_recv()
+            keep_copy(c, n).wait()
         return carry
 
     lax.fori_loop(0, half, drain, 0)
+
+
+def deliver(*refs):
+    *refs, held, arrive, sem = refs
+    count = len(refs) // 2
+    rows = refs[0].shape[0] // PIECES
+    copies = []
+    loads = []
+    for n in range(count):
+        for piece in range(PIECES):
+            part = pl.ds(piece * rows, rows)
+            here = held.at[n, part]
+            loads.append(pltpu.make_async_copy(refs[n].at[part], here, arrive.at[n, piece]))
+            copies.append(
+                pltpu.make_async_copy(here, refs[count + n].at[part], sem.at[n, piece])
+            )
+    for load in loads:
+        load.start()
+    for load, copy in zip(loads, copies):
+        load.wait()
+        copy.start()
+    for copy in copies:
+        copy.wait()
 
 
 def shards(queries, keys, values, out_grad, pair_mask):
@@ -357,12 +390,11 @@
     dma = pltpu.SemaphoreType.DMA
     flops = 2 * rows * rows * HDIM * 5 * 10 * half
     out = jax.ShapeDtypeStruct((rows, width), low)
-    vmem = pl.BlockSpec(memory_space=pltpu.VMEM)
-    return pl.pallas_call(
+    results = pl.pallas_call(
         functools.partial(kernel, half, pairs),
         out_shape=(out, out, out),
         in_specs=[pl.BlockSpec(memory_space=pltpu.SMEM)] + [pl.BlockSpec(memory_space=pl.ANY)] * 4,
-        out_specs=(vmem, vmem, vmem),
+        out_specs=(pl.BlockSpec(memory_space=pl.ANY),) * 3,
         scratch_shapes=[
             pltpu.VMEM((half, 6, 2, rows, HDIM), low),
             pltpu.VMEM((half, 2, 2, rows, HDIM), low),
@@ -371,6 +403,7 @@
             pltpu.VMEM((half, 2, rows, HDIM), full),
             pltpu.VMEM((half, 2, 2, rows, HDIM), low),
             pltpu.VMEM((half, rows, HDIM), low),
+            pltpu.VMEM((half, rows, HDIM), low),
             pltpu.VMEM((half, 4, rows), full),
             pltpu.VMEM((half, 2, 4, rows), full),
             pltpu.VMEM((half, 2, 4, rows), full),
@@ -378,6 +411,7 @@
             pltpu.VMEM((half, 2, 4, rows), full),
             pltpu.VMEM((2, 2, 5, rows, rows), full),
             pltpu.VMEM((2, 2, 5, rows, rows), full),
+            dma((half, 3)),
             dma((half, 4)),
             dma((half, 4)),
             dma((half, 4)),
@@ -399,6 +433,21 @@
             collective_id=0, has_side_effects=True, vmem_limit_bytes=60 * 1024 * 1024
         ),
     )(pair_mask, queries, keys, values, out_grad)
+    anywhere = pl.BlockSpec(memory_space=pl.ANY)
+    return pl.pallas_call(
+        deliver,
+        out_shape=(out, out, out),
+        in_specs=[anywhere] * 3,
+        out_specs=(pl.BlockSpec(memory_space=pl.ANY),) * 3,
+        scratch_shapes=[
+            pltpu.VMEM((3, rows, width), low),
+            dma((3, PIECES)),
+            dma((3, PIECES)),
+        ],
+        cost_estimate=pl.CostEstimate(
+            flops=0, bytes_accessed=12 * rows * width, transcendentals=0
+        ),
+    )(*results)
 
 
 def solution(mesh):

time: 67.5 us -> 63.8 us (0.945)
  local copies, waits for them, and re-layouts: 4.19 us -> 0 us
    unnamed x7 -> x0, local copies, waits for them, and re-layouts: 4.19 us -> none
    pallas_call x0 -> x1, Pallas kernels: none -> 2.34 us  [shards(): pl.pallas_call(deliver, out_shape=(out, out, out), in_specs=[anywhere] *...]
    pallas_call x1, Pallas kernels: 62.5 us -> 60.7 us  [shards(): pl.pallas_call(functools.partial(kernel, half, pairs), out_shape=(out, ou...]
where the time goes in v4:
time: 63.8 us; the launch traced here: 63.6 us
  Pallas kernels  63 us (99%)
  between operations  0.64 us (1%)
    pallas_call x1, Pallas kernels, shards(): pl.pallas_call(functools.partial(kernel, half, pairs), out_shape=(out, ou...  60.7 us
    pallas_call x1, Pallas kernels, shards(): pl.pallas_call(deliver, out_shape=(out, out, out), in_specs=[anywhere] *...  2.34 us

profile of v4, /device:TPU:0, one launch (start us, length us, event | category | flops | bytes accessed | tf_op | source)
XLA Modules:
  0.0 63.6 jit_solution(8647384271958157481)
XLA Ops:
  0.6 60.7 %shard_map.76 = (bf16[256,1280]{1,0:T(8,128)(2,1)}, bf16[256,1280]{1,0:T(8,128)(2,1)}, bf16[256,1280]{1,0:T(8,128)(2,1)}) custom-call(s32[8,5]{1,0:T(8,128)} %mask_ref.1, bf16[256,1280]{1,0:T(8,128)(2,1)} %q_ref.1, bf16[256,1280]{1,0:T(8,128)(2,1)} %k_ref.1, bf16[256,1280]{1,0:T(8,128)(2,1)} %v_ref.1, bf16[256,1280]{1,0:T(8,128)(2,1)} %g_ref.1), custom_call_target="tpu_custom_call" | custom-call | flops 4194304000 | bytes 4587520 | tf_op jit(solution)/shard_map/pallas_call | solution.py:393
  61.3 2.3 %shard_map.77 = (bf16[256,1280]{1,0:T(8,128)(2,1)}, bf16[256,1280]{1,0:T(8,128)(2,1)}, bf16[256,1280]{1,0:T(8,128)(2,1)}) custom-call(bf16[256,1280]{1,0:T(8,128)(2,1)} %get-tuple-element.6.refs_0_, bf16[256,1280]{1,0:T(8,128)(2,1)} %get-tuple-element.7.refs_1_, bf16[256,1280]{1,0:T(8,128)(2,1)} %get-tuple-element.8.refs_2_), custom_call_target="tpu_custom_call" | custom-call | bytes 3932160 | tf_op jit(solution)/shard_map/pallas_call | solution.py:437

commit v5 on v4

--- a/solution.py
+++ b/solution.py
@@ -192,18 +192,28 @@
     pl.semaphore_wait(barrier, 1 + has_left.astype(jnp.int32) + has_right.astype(jnp.int32))
 
     def launch(c, carry):
-        for n in range(4):
-            x_copy(c, n, par).start()
+        for n in range(2):
+
+            @pl.when(c < half)
+            def _():
+                x_copy(c, n, par).start()
+
+        for n in range(2, 4):
+
+            @pl.when(c >= 1)
+            def _():
+                x_copy(c - 1, n, par).start()
+
         return carry
 
-    lax.fori_loop(0, half, launch, 0)
+    lax.fori_loop(0, half + 1, launch, 0)
 
     def send_own(c):
         for n in range(2):
             own_copy(c, n).wait()
         each_side(lambda side, to: z_copy(c, side, par, to).start())
 
-    ahead = min(2, half)
+    ahead = min(3, half)
 
     def forward(c):
         for n in range(2):
@@ -219,7 +229,7 @@
 
     def first(c):
         now = lax.rem(c, 2)
-        for slot in range(6):
+        for slot in (0, 1, 4, 5, 2, 3):
             q = near[c, slot, 0]
             g = near[c, slot, 1]
             frame = lax.rem(2 * pair + 2 * pairs - 2 + slot, 2 * pairs)
@@ -243,6 +253,8 @@
             else:
                 part[c, slot // 4, row : row + 1] = total
                 part[c, slot // 4, row + 1 : row + 2] = mixed
+            if slot == 5:
+                each_side(lambda side, to: p_copy(c, side, to).start())
 
     def combine(c):
         each_side(lambda side, to: p_arrival(c, side).wait_recv())
@@ -258,7 +270,7 @@
         each_side(lambda side, to: s_arrival(c, side).wait_recv())
         dk = [None, None]
         dv = [None, None]
-        for slot in range(6):
+        for slot in (0, 1, 4, 5, 2, 3):
             row = 2 * (slot % 2)
             held = stat[c] if 2 <= slot < 4 else stat_in[c, slot // 4]
             inverse = held[row : row + 1]
@@ -283,7 +295,8 @@
                 acc[c, slot - 2] = dq
             else:
                 ret[c, slot // 4, slot % 2] = dq.astype(jnp.bfloat16)
-        each_side(lambda side, to: r_copy(c, side, to).start())
+            if slot == 5:
+                each_side(lambda side, to: r_copy(c, side, to).start())
         for f in range(2):
             kvs[c, f, 0] = (dk[f] * scale).astype(jnp.bfloat16)
             kvs[c, f, 1] = dv[f].astype(jnp.bfloat16)
@@ -321,7 +334,6 @@
             for frame in range(2):
                 each_side(lambda side, to: z_arrival(c, side, frame).wait_recv())
             first(c)
-            each_side(lambda side, to: p_copy(c, side, to).start())
 
         @pl.when(c + 1 < half)
         def _():

time: 63.8 us -> 63.4 us (level)
  no operation moved by 1% of the time
where the time goes in v5:
time: 63.4 us; the launch traced here: 63.2 us
  Pallas kernels  62.5 us (99%)
  between operations  0.64 us (1%)
    pallas_call x1, Pallas kernels, shards(): pl.pallas_call(functools.partial(kernel, half, pairs), out_shape=(out, ou...  60.2 us
    pallas_call x1, Pallas kernels, shards(): pl.pallas_call(deliver, out_shape=(out, out, out), in_specs=[anywhere] *...  2.34 us

profile of v5, /device:TPU:0, one launch (start us, length us, event | category | flops | bytes accessed | tf_op | source)
XLA Modules:
  0.0 63.2 jit_solution(6070145517574734861)
XLA Ops:
  0.6 60.2 %shard_map.76 = (bf16[256,1280]{1,0:T(8,128)(2,1)}, bf16[256,1280]{1,0:T(8,128)(2,1)}, bf16[256,1280]{1,0:T(8,128)(2,1)}) custom-call(s32[8,5]{1,0:T(8,128)} %mask_ref.1, bf16[256,1280]{1,0:T(8,128)(2,1)} %q_ref.1, bf16[256,1280]{1,0:T(8,128)(2,1)} %k_ref.1, bf16[256,1280]{1,0:T(8,128)(2,1)} %v_ref.1, bf16[256,1280]{1,0:T(8,128)(2,1)} %g_ref.1), custom_call_target="tpu_custom_call" | custom-call | flops 4194304000 | bytes 4587520 | tf_op jit(solution)/shard_map/pallas_call | solution.py:405
  60.8 2.3 %shard_map.77 = (bf16[256,1280]{1,0:T(8,128)(2,1)}, bf16[256,1280]{1,0:T(8,128)(2,1)}, bf16[256,1280]{1,0:T(8,128)(2,1)}) custom-call(bf16[256,1280]{1,0:T(8,128)(2,1)} %get-tuple-element.6.refs_0_, bf16[256,1280]{1,0:T(8,128)(2,1)} %get-tuple-element.7.refs_1_, bf16[256,1280]{1,0:T(8,128)(2,1)} %get-tuple-element.8.refs_2_), custom_call_target="tpu_custom_call" | custom-call | bytes 3932160 | tf_op jit(solution)/shard_map/pallas_call | solution.py:449
